TPU v7x, 256 devices: a whole 4x4x8 slice. The times are simulated.
256 devices in a mesh: batch: 4 (over y), patch: 16 (over z_hi, x, core), tensor: 4 (over z_lo).
Axes of the slice: x: 4, y: 4, z: 8 (z_hi: 2, z_lo: 4; z = z_hi * 4 + z_lo), core: 2. Of those that a mesh axis runs over, the one named last changes fastest.
Arguments:
- image: bfloat16 [32768, 3072], P(('batch', 'patch'), 'tensor'), parts along dimension 0, may hold values from -6 to 6
- modulation: float32 [12, 3072], P('batch'), parts along dimension 0, may hold values from -4 to 4
- w_query: bfloat16 [3072, 1536], P(None, 'tensor'), may hold values from -0.109375 to 0.109375
- w_key: bfloat16 [3072, 1536], P(None, 'tensor'), may hold values from -0.109375 to 0.109375
- w_value: bfloat16 [3072, 1536], P(None, 'tensor'), may hold values from -0.109375 to 0.109375
- w_out: bfloat16 [1536, 3072], P('tensor'), may hold values from -0.15625 to 0.15625
- query_gain: float32 [128], replicated, may hold values from 1.2 to 3
- key_gain: float32 [128], replicated, may hold values from 1.2 to 3
- text_keys: bfloat16 [2048, 1536], P('batch', 'tensor'), parts along dimension 0, may hold values from -12 to 12
- text_values: bfloat16 [2048, 1536], P('batch', 'tensor'), parts along dimension 0, may hold values from -6 to 6
- stale_keys: bfloat16 [32768, 1536], P(('batch', 'patch'), 'tensor'), parts along dimension 0, may hold values from -48 to 48, as said below
- stale_values: bfloat16 [32768, 1536], P(('batch', 'patch'), 'tensor'), parts along dimension 0, may hold values from -6 to 6
Outputs:
- update: bfloat16 [32768, 3072], P(('batch', 'patch'), 'tensor'), parts along dimension 0
There are 4 independent parts, one for each index of `batch`. A program takes and returns all parts, laid end to end along the dimension named above; an argument that names none is the same for every part. Nothing has to cross between parts.
Inputs may be any that keep to these rules, and one draw needn't show every extreme that they name: `stale_keys`: cached keys of the previous step.
All inputs are finite; a program needn't handle non-finite values.
Results may differ from a plain program's by a relative error of at most 0.017.
Values may be sent and summed in bfloat16 or wider, within the bound.
A program may use at most 128 MiB of HBM per device.

v0:
```python
import math

import jax
import jax.numpy as jnp
from jax import lax
from jax.sharding import PartitionSpec as P


def modulate(whole_rows, modulation):
    values = whole_rows.astype(jnp.float32)
    row_mean = jnp.mean(values, axis=-1, keepdims=True)
    centred = values - row_mean
    variance = jnp.mean(centred * centred, axis=-1, keepdims=True)
    normed = centred * lax.rsqrt(variance + 1e-06)
    return (normed * (1.0 + modulation[1]) + modulation[0]).astype(jnp.bfloat16)


def head_norm(projected, gain, head_width):
    heads_view = projected.reshape(projected.shape[0], -1, head_width)
    power = jnp.mean(heads_view * heads_view, axis=-1, keepdims=True)
    return (heads_view * lax.rsqrt(power + 1e-06) * gain).astype(jnp.bfloat16)


def shards(
    image,
    modulation,
    w_query,
    w_key,
    w_value,
    w_out,
    query_gain,
    key_gain,
    text_keys,
    text_values,
    stale_keys,
    stale_values,
):
    rows_here = image.shape[0]
    head_width = query_gain.shape[0]
    heads_here = w_query.shape[1] // head_width
    whole_rows = lax.all_gather(image, "tensor", axis=1, tiled=True)
    modulated = modulate(whole_rows, modulation)
    query = head_norm(
        jnp.dot(modulated, w_query, preferred_element_type=jnp.float32), query_gain, head_width
    )
    keys_new = head_norm(
        jnp.dot(modulated, w_key, preferred_element_type=jnp.float32), key_gain, head_width
    )
    values_new = (
        jnp.dot(modulated, w_value, preferred_element_type=jnp.float32)
        .astype(jnp.bfloat16)
        .reshape(rows_here, heads_here, head_width)
    )
    score_scale = 1.0 / math.sqrt(head_width)
    fresh_keys = jnp.concatenate([text_keys.reshape(-1, heads_here, head_width), keys_new], 0)
    fresh_values = jnp.concatenate([text_values.reshape(-1, heads_here, head_width), values_new], 0)
    scores = (
        jnp.einsum("qhd,khd->hqk", query, fresh_keys, preferred_element_type=jnp.float32)
        * score_scale
    )
    start_max = jnp.max(scores, axis=-1)
    expo = jnp.exp(scores - start_max[..., None])
    start_total = jnp.sum(expo, axis=-1)
    start_acc = jnp.einsum(
        "hqk,khd->hqd", expo.astype(jnp.bfloat16), fresh_values, preferred_element_type=jnp.float32
    )
    own_index = lax.axis_index("patch")
    key_rows = lax.all_gather(stale_keys, "patch", axis=0, tiled=True)
    value_rows = lax.all_gather(stale_values, "patch", axis=0, tiled=True)
    count = key_rows.shape[0]
    width = math.gcd(math.gcd(count, rows_here), 512)
    blocks = count // width
    key_blocks = key_rows.reshape(blocks, width, heads_here, head_width)
    value_blocks = value_rows.reshape(blocks, width, heads_here, head_width)
    offsets = jnp.arange(blocks, dtype=jnp.int32) * width

    def advance(state, blocked):
        keys_block, values_block, first_row = blocked
        run_max, run_total, run_acc = state
        block_scores = (
            jnp.einsum("qhd,khd->hqk", query, keys_block, preferred_element_type=jnp.float32)
            * score_scale
        )
        block_scores = jnp.where(first_row // rows_here == own_index, -1e30, block_scores)
        new_max = jnp.maximum(run_max, jnp.max(block_scores, axis=-1))
        shrink = jnp.exp(run_max - new_max)
        block_expo = jnp.exp(block_scores - new_max[..., None])
        new_total = run_total * shrink + jnp.sum(block_expo, axis=-1)
        new_acc = run_acc * shrink[..., None] + jnp.einsum(
            "hqk,khd->hqd",
            block_expo.astype(jnp.bfloat16),
            values_block,
            preferred_element_type=jnp.float32,
        )
        return ((new_max, new_total, new_acc), None)

    result, unused = lax.scan(
        advance, (start_max, start_total, start_acc), (key_blocks, value_blocks, offsets)
    )
    final_max, final_total, final_acc = result
    attended = (
        jnp.transpose(final_acc / final_total[..., None], (1, 0, 2))
        .reshape(rows_here, heads_here * head_width)
        .astype(jnp.bfloat16)
    )
    feature_width = w_out.shape[1] // lax.axis_size("tensor")
    gate_row = lax.dynamic_slice_in_dim(
        modulation[2], lax.axis_index("tensor") * feature_width, feature_width, 0
    )
    partial_terms = jnp.dot(attended, w_out, preferred_element_type=jnp.float32)
    projected = lax.psum_scatter(
        partial_terms.astype(jnp.bfloat16), "tensor", scatter_dimension=1, tiled=True
    ).astype(jnp.float32)
    return (gate_row * projected).astype(jnp.bfloat16)


def solution(mesh):
    in_specs = (
        P(("batch", "patch"), "tensor"),
        P("batch", None),
        P(None, "tensor"),
        P(None, "tensor"),
        P(None, "tensor"),
        P("tensor", None),
        P(),
        P(),
        P("batch", "tensor"),
        P("batch", "tensor"),
        P(("batch", "patch"), "tensor"),
        P(("batch", "patch"), "tensor"),
    )
    out_specs = P(("batch", "patch"), "tensor")
    return jax.shard_map(shards, mesh=mesh, in_specs=in_specs, out_specs=out_specs, check_vma=False)
```

profile of v0, /device:TPU:1, one launch (start us, length us, event | category | flops | bytes accessed | tf_op | source)
XLA Modules:
  0.0 498.1 jit_solution(5610051005933175643)
XLA Ops:
  13.2 66.4 %all-gather.4.cloned.1.call-done = bf16[512,3072]{1,0:T(8,128)(2,1)} async-done(((bf16[512,768]{1,0:T(8,128)(2,1)}), bf16[512,3072]{1,0:T(8,128)(2,1)}) %all-gather.4.cloned.1.call-update) | async-done | bytes 3145744 | tf_op jit(solution)/shard_map/all_gather | solution.py:41
  79.6 2.5 convert_reduce_fusion
  88.0 4.9 fusion.45
  94.4 4.4 convolution_convert_fusion.1
  108.7 67.4 %all-gather.6.cloned.1.call-done = bf16[8192,384]{1,0:T(8,128)(2,1)} async-done(((bf16[512,384]{1,0:T(8,128)(2,1)}), bf16[8192,384]{1,0:T(8,128)(2,1)}) %all-gather.6.cloned.1.call-update) | async-done | bytes 6291472 | tf_op jit(solution)/shard_map/all_gather | solution.py:68
  176.1 16.7 %reshape.66 = bf16[16,512,3,128]{3,2,1,0:T(4,128)(2,1)} reshape(bf16[8192,384]{1,0:T(8,128)(2,1)} %all-gather.6.cloned.1.call-done) | data formatting | bytes 12582912 | tf_op jit(solution)/shard_map/reshape | solution.py:73
  192.8 7.7 %copy.27 = bf16[16,512,3,128]{3,1,2,0:T(8,128)(2,1)} copy(bf16[16,512,3,128]{3,2,1,0:T(4,128)(2,1)} %reshape.66) | data formatting | bytes 12582912 | tf_op jit(solution)/shard_map/while | solution.py:97
  200.5 66.5 %all-gather.8.cloned.1.call-done = bf16[8192,384]{1,0:T(8,128)(2,1)} async-done(((bf16[512,384]{1,0:T(8,128)(2,1)}), bf16[8192,384]{1,0:T(8,128)(2,1)}) %all-gather.8.cloned.1.call-update) | async-done | bytes 6291472 | tf_op jit(solution)/shard_map/all_gather | solution.py:69
  267.0 16.6 %reshape.67 = bf16[16,512,3,128]{3,2,1,0:T(4,128)(2,1)} reshape(bf16[8192,384]{1,0:T(8,128)(2,1)} %all-gather.8.cloned.1.call-done) | data formatting | bytes 12582912 | tf_op jit(solution)/shard_map/reshape | solution.py:74
  283.7 7.9 %copy.28 = bf16[16,512,3,128]{3,1,2,0:T(8,128)(2,1)} copy(bf16[16,512,3,128]{3,2,1,0:T(4,128)(2,1)} %reshape.67) | data formatting | bytes 12582912 | tf_op jit(solution)/shard_map/while | solution.py:97
  291.5 131.7 %while.16 = (s32[]{:T(128)}, f32[3,512]{1,0:T(4,128)S(1)}, f32[3,512]{1,0:T(4,128)S(1)}, f32[3,512,128]{2,1,0:T(8,128)S(1)}, s32[16]{0:T(128)}, /*index=5*/s32[]...) while((s32[]{:T(128)}, f32[3,512]{1,0:T(4,128)S(1)}, ...), condition=%wide.region_9.10_spmd, body=%wide.region_6.9_spmd.sunk | while | flops 411700224 | bytes 12289331 | solution.py:97
  314.0 2.1 fusion.65
  322.3 2.1 fusion.65
  338.7 2.1 fusion.65
  347.0 2.1 fusion.65
  355.2 2.1 fusion.65
  363.4 2.1 fusion.65
  371.7 2.1 fusion.65
  379.9 2.1 fusion.65
  388.1 2.1 fusion.65
  396.4 2.1 fusion.65
  404.6 2.1 fusion.65
  425.6 3.5 convolution_convert_fusion
  429.8 59.6 %reduce-scatter.2.cloned.1.call-done = bf16[512,768]{1,0:T(8,128)(2,1)} async-done(((bf16[512,3072]{1,0:T(8,128)(2,1)}), bf16[512,768]{1,0:T(8,128)(2,1)}) %reduce-scatter.2.cloned.1.call-update) | async-done | bytes 786448 | tf_op jit(solution)/shard_map/reduce_scatter | solution.py:111
  (160 shorter events, 94.5 us)
Async XLA Ops:
  6.5 419.1 %copy-start = (bf16[384,3072]{1,0:T(8,128)(2,1)S(1)}, bf16[384,3072]{1,0:T(8,128)(2,1)}, u32[]{:S(2)}) copy-start(bf16[384,3072]{1,0:T(8,128)(2,1)} %param.19) | copy-start | bytes 7077892
  6.5 4.4 copy-start.5
  6.5 6.0 %copy-start.8 = (f32[3,3072]{1,0:T(4,128)S(1)}, f32[3,3072]{1,0:T(4,128)}, u32[]{:S(2)}) copy-start(f32[3,3072]{1,0:T(4,128)} %param.15) | copy-start | bytes 110596
  6.5 73.0 %all-gather.4.cloned.1.call-start = ((), (), s32[]{:S(2)}) async-start(), calls=%async_computation.1 | async-start | bytes 3932160 | tf_op jit(solution)/shard_map/all_gather | solution.py:41
  7.3 168.9 %all-gather.6.cloned.1.call-start = ((), (), s32[]{:S(2)}) async-start(), calls=%async_computation.2 | async-start | bytes 6684672 | tf_op jit(solution)/shard_map/all_gather | solution.py:68
  8.0 259.0 %all-gather.8.cloned.1.call-start = ((), (), s32[]{:S(2)}) async-start(), calls=%async_computation.3 | async-start | bytes 6684672 | tf_op jit(solution)/shard_map/all_gather | solution.py:69
  8.7 480.7 %reduce-scatter.2.cloned.1.call-start = ((), (), s32[]{:S(2)}) async-start(), calls=%async_computation.4 | async-start | bytes 3932160 | tf_op jit(solution)/shard_map/reduce_scatter | solution.py:111
  79.6 2.8 copy-start.1
  83.4 1.8 copy-start.11
  85.2 1.7 copy-start.3
  86.9 6.1 %copy-start.2 = (f32[512,384]{0,1:T(8,128)}, f32[512,384]{0,1:T(8,128)S(1)}, u32[]{:S(2)}) copy-start(f32[512,384]{0,1:T(8,128)S(1)} %fusion.44) | copy-start | bytes 2359300
  94.4 7.8 %copy-start.9 = (f32[128]{0:T(128)S(1)}, f32[128]{0:T(128)}, u32[]{:S(2)}) copy-start(f32[128]{0:T(128)} %param.20) | copy-start | bytes 1540
  98.8 4.9 copy-start.10
  106.0 1.4 copy-start.6
  106.0 1.4 copy-start.7
  423.2 0.9 copy-start.4
Sparse Core Ops, SparseCore 0:
  9.2 70.3 all-gather.3
  82.3 93.7 all-gather.5
  178.9 88.1 all-gather.7
  429.3 60.1 reduce-scatter.1
where the time goes:
time: 501 us; the launch traced here: 498 us
  waiting for transfers between devices  262 us (52%)
  local copies, waits for them, and re-layouts  78 us (16%)
  matrix products  77.3 us (15%)
  loops' own time  42.5 us (8%)
  other arithmetic  24.7 us (5%)
  between operations  13.4 us (3%)
    all_gather x1, waiting for transfers between devices, shards(): key_rows = lax.all_gather(stale_keys, 'patch', axis=0, tiled=True)  67.4 us
    all_gather x1, waiting for transfers between devices, shards(): value_rows = lax.all_gather(stale_values, 'patch', axis=0, tiled=True)  66.5 us
    all_gather x1, waiting for transfers between devices, shards(): whole_rows = lax.all_gather(image, 'tensor', axis=1, tiled=True)  66.4 us
    reduce_scatter x1, waiting for transfers between devices, shards(): lax.psum_scatter(partial_terms.astype(jnp.bfloat16), 'tensor', scatter_di...  59.6 us
    another operation x1, loops' own time, shards(): lax.scan(advance, (start_max, start_total, start_acc), (key_blocks, value...  42.5 us
    dot_general x16, matrix products, advance(): jnp.einsum('hqk,khd->hqd', block_expo.astype(jnp.bfloat16), values_block,...  34.3 us
    dot_general x16, matrix products, advance(): jnp.einsum('qhd,khd->hqk', query, keys_block, preferred_element_type=jnp....  25.4 us
    dynamic_slice x16, local copies, waits for them, and re-layouts, shards(): lax.scan(advance, (start_max, start_total, start_acc), (key_blocks, value...  18.9 us
  transfers between devices with their start and end apart: 4, of which 4 were waited for; matrix products, arithmetic and copies ran while one was open for 12% of the time, Pallas kernels for 0%

commit v1 on v0

v1 whole, which is shorter than its diff:
```python
import functools
import math

import jax
import jax.numpy as jnp
from jax import lax
from jax.experimental import pallas as pl
from jax.experimental.pallas import tpu as pltpu
from jax.sharding import PartitionSpec as P

MESH = pl.DeviceIdType.MESH
BF = jnp.bfloat16
F32 = jnp.float32
ROWS = 512
HW = 128
HEADS = 3
WIDE = HEADS * HW
SLICE = 768
DM = 4 * SLICE
CH = 128
NCH = ROWS // CH
KB = 2048
PIECES = 2
LOG2E = 1.4426950408889634

KV_NEAR = 0
KV_TWO = KV_NEAR + 4
KV_SIB = KV_TWO + 2
KV_Z = KV_SIB + 8
KV_FX = KV_Z + 2 * PIECES
KV_FTWO = KV_FX + 4 * PIECES
KV_FSIB = KV_FTWO + 2 * PIECES
W_A = KV_FSIB + 8 * PIECES
W_B = W_A + 3
W_C = W_B + 3
W_D = W_C + 3
O_A = W_D + 1
O_B = O_A + 4
O_C = O_B + 3
O_D = O_C + 3
IMG = O_D + 1
QKV = IMG + 4 * NCH
TAIL = QKV + 3 * NCH
OUT = TAIL + 4 * NCH
NSEM = OUT + NCH


def kernel(
    img_h, mod, wq_h, wk_h, wv_h, wo_h, qgain, kgain, tk_h, tv_h, sk_h, sv_h,
    out,
    kbuf, vbuf, img, w_own, w_end, w_o, modl, qbuf, stage, att, ostage, m_s, acc_s,
    ssem, rsem, lsem,
):
    yy = lax.axis_index("batch")
    patch = lax.axis_index("patch")
    t = lax.axis_index("tensor")
    zh = patch // 8
    xx = lax.rem(patch, 8) // 2
    cc = lax.rem(patch, 2)
    is_mid = (t == 1) | (t == 2)
    is_end = (t == 0) | (t == 3)
    pair = jnp.where(t < 2, 1 - t, 5 - t)

    def at_x(d):
        return {"patch": zh * 8 + lax.rem(xx + d + 4, 4) * 2 + cc}

    def at_y(d):
        return {"batch": lax.rem(yy + d + 4, 4)}

    sib = {"patch": zh * 8 + xx * 2 + (1 - cc)}
    far = {"patch": (1 - zh) * 8 + xx * 2 + cc}
    to_pair = {"tensor": pair}

    def copy(src, dst, i, dev):
        return pltpu.make_async_remote_copy(
            src_ref=src, dst_ref=dst, send_sem=ssem.at[i], recv_sem=rsem.at[i],
            device_id=dev, device_id_type=MESH,
        )

    def got(dst, i):
        copy(dst, dst, i, sib).wait_recv()

    def sent(src, i):
        copy(src, src, i, sib).wait_send()

    def block(buf, slot, piece=0, pieces=1):
        n = ROWS // pieces
        return buf.at[pl.ds(slot * ROWS + piece * n, n)]

    local = [
        pltpu.make_async_copy(wq_h, w_own.at[0], lsem.at[0]),
        pltpu.make_async_copy(wk_h, w_own.at[1], lsem.at[1]),
        pltpu.make_async_copy(wv_h, w_own.at[2], lsem.at[2]),
        pltpu.make_async_copy(tk_h, block(kbuf, 0), lsem.at[3]),
        pltpu.make_async_copy(tv_h, block(vbuf, 0), lsem.at[4]),
        pltpu.make_async_copy(img_h, img.at[t], lsem.at[5]),
    ]
    my_cols = pl.ds(pl.multiple_of(t * SLICE, SLICE), SLICE)
    pair_cols = pl.ds(pl.multiple_of(pair * SLICE, SLICE), SLICE)
    local_o = [
        pltpu.make_async_copy(wo_h.at[:, my_cols], w_o.at[0, :, pl.ds(0, SLICE)], lsem.at[6]),
        pltpu.make_async_copy(wo_h.at[:, pair_cols], w_o.at[0, :, pl.ds(SLICE, SLICE)], lsem.at[7]),
    ]

    peers = [sib, far] + [at_x(d) for d in (1, 2, 3)] + [at_y(d) for d in (1, 2, 3)]
    peers += [{"tensor": lax.rem(t + d, 4)} for d in (1, 2, 3)]
    barrier = pltpu.get_barrier_semaphore()
    for p in peers:
        pl.semaphore_signal(barrier, inc=1, device_id=p, device_id_type=MESH)
    pl.semaphore_wait(barrier, len(peers))

    stale = (sk_h, sv_h)
    bufs = (kbuf, vbuf)

    def z_piece(j, p):
        n = ROWS // PIECES
        return copy(
            stale[j].at[pl.ds(p * n, n)], block(bufs[j], 8, p, PIECES), KV_Z + j * PIECES + p, far
        )

    for p in range(PIECES):
        for j in range(2):
            z_piece(j, p).start()

    w_rows = pl.ds(pl.multiple_of(cc * 1536 + yy * 384 + xx * 96, 96), 96)

    def w_a(j):
        return copy((wq_h, wk_h, wv_h)[j].at[w_rows], w_end.at[j, w_rows], W_A + j, to_pair)

    @pl.when(is_end)
    def _():
        for j in range(3):
            w_a(j).start()

    def img_copy(m, c):
        r = lax.rem(t - m + 4, 4)
        rows = pl.ds(pl.multiple_of(c * CH, CH), CH)
        return copy(img_h.at[rows], img.at[t, rows], IMG + r * NCH + c, {"tensor": jnp.int32(m)})

    def start_img(c):
        for m in (1, 2):
            @pl.when(t != m)
            def _(m=m):
                img_copy(m, c).start()

    for c in range(NCH):
        start_img(c)

    for j in range(2):
        copy(stale[j], block(bufs[j], 2), KV_NEAR + 2 * j, at_x(-1)).start()
        copy(stale[j], block(bufs[j], 4), KV_NEAR + 2 * j + 1, at_x(1)).start()
    for j in range(2):
        copy(stale[j], block(bufs[j], 1), KV_SIB + 4 * j, sib).start()

    for cp in local:
        cp.start()

    @pl.when(is_mid)
    def _():
        for cp in local_o:
            cp.start()

    o_rows = pl.ds(pl.multiple_of(cc * 192 + yy * 48, 48), 48)
    o_cols = pl.ds(pl.multiple_of(xx * 384, 384), 384)

    def o_a(m):
        r = lax.rem(t - m + 4, 4)
        e = 3 * (m - 1)
        start = jnp.where(xx < 2, m, e) * SLICE + lax.rem(xx, 2) * 384
        src = wo_h.at[o_rows, pl.ds(pl.multiple_of(start, 384), 384)]
        return copy(src, w_o.at[r, o_rows, o_cols], O_A + r, {"tensor": jnp.int32(m)})

    for m in (1, 2):
        @pl.when(t != m)
        def _(m=m):
            o_a(m).start()

    m_s[...] = jnp.full(m_s.shape, -1e30, F32)
    acc_s[...] = jnp.zeros(acc_s.shape, F32)

    def w_b(d):
        piece = w_end.at[:, w_rows]
        return copy(piece, piece, W_B + d - 1, at_x(d))

    def w_c(d):
        rows = pl.ds(pl.multiple_of(cc * 1536 + yy * 384, 384), 384)
        piece = w_end.at[:, rows]
        return copy(piece, piece, W_C + d - 1, at_y(d))

    def w_d():
        piece = w_end.at[:, pl.ds(pl.multiple_of(cc * 1536, 1536), 1536)]
        return copy(piece, piece, W_D, sib)

    def o_b(d):
        piece = w_o.at[pl.ds(1, 3), o_rows, o_cols]
        return copy(piece, piece, O_B + d - 1, at_x(d))

    def o_c(d):
        piece = w_o.at[pl.ds(1, 3), o_rows]
        return copy(piece, piece, O_C + d - 1, at_y(d))

    def o_d():
        piece = w_o.at[pl.ds(1, 3), pl.ds(pl.multiple_of(cc * 192, 192), 192)]
        return copy(piece, piece, O_D, sib)

    def wait_w_b():
        for d in (1, 2, 3):
            rows = pl.ds(pl.multiple_of(cc * 1536 + yy * 384 + lax.rem(xx - d + 4, 4) * 96, 96), 96)
            got(w_end.at[:, rows], W_B + d - 1)

    def wait_w_c():
        for d in (1, 2, 3):
            rows = pl.ds(pl.multiple_of(cc * 1536 + lax.rem(yy - d + 4, 4) * 384, 384), 384)
            got(w_end.at[:, rows], W_C + d - 1)

    def wait_o_b():
        for d in (1, 2, 3):
            cols = pl.ds(pl.multiple_of(lax.rem(xx - d + 4, 4) * 384, 384), 384)
            got(w_o.at[pl.ds(1, 3), o_rows, cols], O_B + d - 1)

    def wait_o_c():
        for d in (1, 2, 3):
            rows = pl.ds(pl.multiple_of(cc * 192 + lax.rem(yy - d + 4, 4) * 48, 48), 48)
            got(w_o.at[pl.ds(1, 3), rows], O_C + d - 1)

    @pl.when(is_mid)
    def _():
        for j in range(3):
            got(w_end.at[j, w_rows], W_A + j)
        for d in (1, 2, 3):
            w_b(d).start()
        for r in (1, 2, 3):
            got(w_o.at[r, o_rows, o_cols], O_A + r)
        for d in (1, 2, 3):
            o_b(d).start()

    def near_sib(j, i):
        src = stale[j] if i == 0 else block(bufs[j], 2 * i)
        return copy(src, block(bufs[j], 2 * i + 1), KV_SIB + 4 * j + i, sib)

    def near_two(j):
        if j == 0:
            return copy(block(kbuf, 4), block(kbuf, 6), KV_TWO, at_x(1))
        return copy(block(vbuf, 2), block(vbuf, 6), KV_TWO + 1, at_x(-1))

    @pl.when(is_mid)
    def _():
        wait_w_b()
        for d in (1, 2, 3):
            w_c(d).start()
        wait_o_b()
        for d in (1, 2, 3):
            o_c(d).start()

    got(block(kbuf, 4), KV_NEAR + 1)
    near_two(0).start()
    got(block(vbuf, 2), KV_NEAR + 2)
    near_two(1).start()
    near_sib(0, 2).start()
    near_sib(1, 1).start()
    got(block(kbuf, 2), KV_NEAR)
    near_sib(0, 1).start()
    got(block(vbuf, 4), KV_NEAR + 3)
    near_sib(1, 2).start()

    @pl.when(is_mid)
    def _():
        wait_w_c()
        w_d().start()
        wait_o_c()
        o_d().start()

    def far_x(j, p, s):
        src = block(bufs[j], 8, p, PIECES)
        dst = block(bufs[j], 10 + 2 * s, p, PIECES)
        return copy(src, dst, KV_FX + (j * PIECES + p) * 2 + s, at_x(-1 if s == 0 else 1))

    def far_two(j, p):
        src = block(bufs[j], 12 if j == 0 else 10, p, PIECES)
        dst = block(bufs[j], 14, p, PIECES)
        return copy(src, dst, KV_FTWO + j * PIECES + p, at_x(1 if j == 0 else -1))

    def far_sib(j, p, i):
        src = block(bufs[j], 8 + 2 * i, p, PIECES)
        dst = block(bufs[j], 9 + 2 * i, p, PIECES)
        return copy(src, dst, KV_FSIB + (j * PIECES + p) * 4 + i, sib)

    for p in range(PIECES):
        for j in range(2):
            got(block(bufs[j], 8, p, PIECES), KV_Z + j * PIECES + p)
            far_x(j, p, 0).start()
            far_x(j, p, 1).start()
            far_sib(j, p, 0).start()

    for j in range(2):
        got(block(bufs[j], 6), KV_TWO + j)
        near_sib(j, 3).start()

    def far_rest():
        for p in range(PIECES):
            for j in range(2):
                for s in (0, 1):
                    got(block(bufs[j], 10 + 2 * s, p, PIECES), KV_FX + (j * PIECES + p) * 2 + s)
                far_two(j, p).start()
                far_sib(j, p, 1).start()
                far_sib(j, p, 2).start()
        for p in range(PIECES):
            for j in range(2):
                got(block(bufs[j], 14, p, PIECES), KV_FTWO + j * PIECES + p)
                far_sib(j, p, 3).start()
        for p in range(PIECES):
            for j in range(2):
                for i in range(4):
                    got(
                        block(bufs[j], 9 + 2 * i, p, PIECES),
                        KV_FSIB + (j * PIECES + p) * 4 + i,
                    )

    def near_rest():
        for j in range(2):
            for i in range(4):
                got(block(bufs[j], 2 * i + 1), KV_SIB + 4 * j + i)

    def chunk_rows(c, base=0):
        return pl.ds(pl.multiple_of(base + c * CH, CH), CH)

    def norm_chunk(c):
        rows = chunk_rows(c)
        total = jnp.zeros((CH, 1), F32)
        for s in range(4):
            total += jnp.sum(img[s, rows].astype(F32), axis=1, keepdims=True)
        mean = total * (1.0 / DM)
        total = jnp.zeros((CH, 1), F32)
        for s in range(4):
            d = img[s, rows].astype(F32) - mean
            total += jnp.sum(d * d, axis=1, keepdims=True)
        rstd = lax.rsqrt(total * (1.0 / DM) + 1e-06)
        for s in range(4):
            cols = slice(s * SLICE, (s + 1) * SLICE)
            d = (img[s, rows].astype(F32) - mean) * rstd
            modl[:, cols] = (d * (1.0 + mod[1:2, cols]) + mod[0:1, cols]).astype(BF)

    def project(w, put):
        for j in range(3):
            y = jnp.dot(modl[...], w[j], preferred_element_type=F32)
            if j == 2:
                put(j, y.astype(BF))
                continue
            gain = qgain[...] * (LOG2E / math.sqrt(HW)) if j == 0 else kgain[...]
            parts = []
            for h in range(HEADS):
                v = y[:, h * HW : (h + 1) * HW]
                power = jnp.mean(v * v, axis=1, keepdims=True)
                parts.append((v * lax.rsqrt(power + 1e-06) * gain).astype(BF))
            put(j, jnp.concatenate(parts, axis=1))

    FRESH = 16 * ROWS

    def qkv_copy(j, c):
        dst = (
            qbuf.at[chunk_rows(c)],
            kbuf.at[chunk_rows(c, FRESH)],
            vbuf.at[chunk_rows(c, FRESH)],
        )[j]
        return copy(stage.at[j, chunk_rows(c)], dst, QKV + j * NCH + c, to_pair)

    def fresh_chunk(c):
        @pl.when(is_mid)
        def _():
            for r in (1, 2, 3):
                s = lax.rem(t + r, 4)
                got(img.at[s, chunk_rows(c)], IMG + r * NCH + c)
            norm_chunk(c)

            def put_end(j, v):
                stage[j, chunk_rows(c)] = v
                qkv_copy(j, c).start()

            project(w_end, put_end)

            def put_own(j, v):
                if j == 0:
                    qbuf[chunk_rows(c)] = v
                else:
                    bufs[j - 1][chunk_rows(c, FRESH)] = v

            project(w_own, put_own)

        @pl.when(is_end)
        def _():
            got(qbuf.at[chunk_rows(c)], QKV + c)
            got(kbuf.at[chunk_rows(c, FRESH)], QKV + NCH + c)
            got(vbuf.at[chunk_rows(c, FRESH)], QKV + 2 * NCH + c)

    def attend(c, start, n):
        rows = chunk_rows(c)
        keys = pl.ds(pl.multiple_of(start, ROWS), n)
        for h in range(HEADS):
            cols = slice(h * HW, (h + 1) * HW)
            k = kbuf[keys, cols]
            v = vbuf[keys, cols]
            s = lax.dot_general(
                qbuf[rows, cols], k, (((1,), (1,)), ((), ())), preferred_element_type=F32
            )
            old = m_s[h, rows]
            new = jnp.maximum(old, jnp.max(s, axis=1, keepdims=True))
            shrink = jnp.exp2(old - new)
            p = jnp.exp2(s - new[:, :1]).astype(BF)
            m_s[h, rows] = new
            both = jnp.concatenate([v, jnp.ones_like(v)], axis=1)
            pv = jnp.dot(p, both, preferred_element_type=F32)
            acc_s[h, rows] = acc_s[h, rows] * jnp.concatenate([shrink, shrink], axis=1) + pv

    def tail_copy(m, c):
        r = lax.rem(t - m + 4, 4)
        rows = chunk_rows(c)
        return copy(att.at[0, rows], att.at[r, rows], TAIL + r * NCH + c, {"tensor": jnp.int32(m)})

    def finish(c):
        attend(c, FRESH, ROWS)
        rows = chunk_rows(c)
        for h in range(HEADS):
            a = acc_s[h, rows]
            att[0, rows, h * HW : (h + 1) * HW] = (a[:, :HW] / a[:, HW:]).astype(BF)
        for m in (1, 2):
            @pl.when(t != m)
            def _(m=m):
                tail_copy(m, c).start()

    for cp in local:
        cp.wait()

    @pl.when(is_mid)
    def _():
        for cp in local_o:
            cp.wait()
        got(w_end.at[:, pl.ds(pl.multiple_of((1 - cc) * 1536, 1536), 1536)], W_D)
        got(w_o.at[pl.ds(1, 3), pl.ds(pl.multiple_of((1 - cc) * 192, 192), 192)], O_D)

    @pl.loop(0, NCH)
    def _(c):
        fresh_chunk(c)

        @pl.when(c == 0)
        def _():
            near_rest()

        @pl.when(c == NCH - 1)
        def _():
            @pl.loop(0, NCH - 1)
            def _(d):
                finish(d)

        @pl.loop(0, 4096 // KB)
        def _(b):
            attend(c, b * KB, KB)

        @pl.when(c == 0)
        def _():
            far_rest()

        @pl.loop(4096 // KB, 8192 // KB)
        def _(b):
            attend(c, b * KB, KB)

    finish(NCH - 1)

    def out_copy(c):
        return copy(ostage.at[chunk_rows(c)], out.at[chunk_rows(c)], OUT + c, to_pair)

    @pl.when(is_mid)
    def _():
        gate_own = mod[2:3, my_cols]
        gate_end = mod[2:3, pair_cols]

        @pl.loop(0, NCH)
        def _(c):
            rows = chunk_rows(c)
            for r in (1, 2, 3):
                got(att.at[r, rows], TAIL + r * NCH + c)
            for half, gate in ((1, gate_end), (0, gate_own)):
                y = jnp.zeros((CH, SLICE), F32)
                for r in range(4):
                    w = w_o[r, :, half * SLICE : (half + 1) * SLICE]
                    y += jnp.dot(att[r, rows], w, preferred_element_type=F32)
                y = (y * gate).astype(BF)
                if half:
                    ostage[rows] = y
                    out_copy(c).start()
                else:
                    out[rows] = y

    @pl.when(is_end)
    def _():
        for c in range(NCH):
            got(out.at[chunk_rows(c)], OUT + c)

    for j in range(2):
        for p in range(PIECES):
            z_piece(j, p).wait_send()
            far_two(j, p).wait_send()
            for s in range(2):
                far_x(j, p, s).wait_send()
            for i in range(4):
                far_sib(j, p, i).wait_send()
        for s in range(2):
            sent(stale[j], KV_NEAR + 2 * j + s)
        for i in range(4):
            near_sib(j, i).wait_send()
        near_two(j).wait_send()

    @pl.when(is_end)
    def _():
        for j in range(3):
            w_a(j).wait_send()

    for m in (1, 2):
        @pl.when(t != m)
        def _(m=m):
            o_a(m).wait_send()
            for c in range(NCH):
                img_copy(m, c).wait_send()
                tail_copy(m, c).wait_send()

    @pl.when(is_mid)
    def _():
        for d in (1, 2, 3):
            w_b(d).wait_send()
            w_c(d).wait_send()
            o_b(d).wait_send()
            o_c(d).wait_send()
        w_d().wait_send()
        o_d().wait_send()
        for c in range(NCH):
            out_copy(c).wait_send()
            for j in range(3):
                qkv_copy(j, c).wait_send()


def shards(image, modulation, w_query, w_key, w_value, w_out, query_gain, key_gain, text_keys, text_values, stale_keys, stale_values):
    hbm = pl.BlockSpec(memory_space=pl.ANY)
    vmem = pl.BlockSpec(memory_space=pltpu.VMEM)
    return pl.pallas_call(
        kernel,
        out_shape=jax.ShapeDtypeStruct((ROWS, SLICE), BF),
        in_specs=[hbm, vmem, hbm, hbm, hbm, hbm, vmem, vmem, hbm, hbm, hbm, hbm],
        out_specs=vmem,
        scratch_shapes=[
            pltpu.VMEM((17 * ROWS, WIDE), BF),
            pltpu.VMEM((17 * ROWS, WIDE), BF),
            pltpu.VMEM((4, ROWS, SLICE), BF),
            pltpu.VMEM((3, DM, WIDE), BF),
            pltpu.VMEM((3, DM, WIDE), BF),
            pltpu.VMEM((4, WIDE, 2 * SLICE), BF),
            pltpu.VMEM((CH, DM), BF),
            pltpu.VMEM((ROWS, WIDE), BF),
            pltpu.VMEM((3, ROWS, WIDE), BF),
            pltpu.VMEM((4, ROWS, WIDE), BF),
            pltpu.VMEM((ROWS, SLICE), BF),
            pltpu.VMEM((HEADS, ROWS, HW), F32),
            pltpu.VMEM((HEADS, ROWS, 2 * HW), F32),
            pltpu.SemaphoreType.DMA((NSEM,)),
            pltpu.SemaphoreType.DMA((NSEM,)),
            pltpu.SemaphoreType.DMA((8,)),
        ],
        compiler_params=pltpu.CompilerParams(
            collective_id=0, has_side_effects=True, vmem_limit_bytes=60 * 1024 * 1024
        ),
        cost_estimate=pl.CostEstimate(
            flops=12_000_000_000, bytes_accessed=20_000_000, transcendentals=14_000_000
        ),
        name="joint_attention",
    )(
        image, modulation, w_query, w_key, w_value, w_out,
        query_gain.reshape(1, HW), key_gain.reshape(1, HW),
        text_keys, text_values, stale_keys, stale_values,
    )


def solution(mesh):
    rows = P(("batch", "patch"), "tensor")
    cols = P(None, "tensor")
    in_specs = (
        rows, P("batch", None), cols, cols, cols, P("tensor", None), P(), P(),
        P("batch", "tensor"), P("batch", "tensor"), rows, rows,
    )
    return jax.shard_map(shards, mesh=mesh, in_specs=in_specs, out_specs=rows, check_vma=False)
```

time: 501 us -> 237 us (0.47)
  waiting for transfers between devices: 262 us -> 0 us
  Pallas kernels: 0 us -> 235 us
  matrix products: 77.3 us -> 0 us
  local copies, waits for them, and re-layouts: 78 us -> 2.06 us
  loops' own time: 42.5 us -> 0 us
  other arithmetic: 24.7 us -> 0 us
  between operations: 13.4 us -> 0.01 us
    pallas_call x0 -> x1, Pallas kernels: none -> 235 us  [shards(): pl.pallas_call(kernel, out_shape=jax.ShapeDtypeStruct((ROWS, SLICE), BF),...]
    all_gather x3 -> x0, waiting for transfers between devices: 200 us -> none  [the longest x1 67.4 us: shards(): key_rows = lax.all_gather(stale_keys, 'patch', axis=0, tiled=True)]
    dot_general x38 -> x0, matrix products: 77.3 us -> none  [the longest x16 34.3 us: advance(): jnp.einsum('hqk,khd->hqd', block_expo.astype(jnp.bfloat16), values_block,...]
    reduce_scatter x1 -> x0, waiting for transfers between devices: 59.6 us -> none  [shards(): lax.psum_scatter(partial_terms.astype(jnp.bfloat16), 'tensor', scatter_di...]
    another operation x1 -> x0, loops' own time: 42.5 us -> none  [shards(): lax.scan(advance, (start_max, start_total, start_acc), (key_blocks, value...]
    reshape x7 -> x0, local copies, waits for them, and re-layouts: 38.6 us -> none  [the longest x1 16.7 us: shards(): key_blocks = key_rows.reshape(blocks, width, heads_here, head_width)]
    dynamic_slice x17 -> x0, local copies, waits for them, and re-layouts: 19.6 us -> none  [the longest x16 18.9 us: shards(): lax.scan(advance, (start_max, start_total, start_acc), (key_blocks, value...]
    reduce_sum x21 -> x0, other arithmetic: 17.4 us -> none  [the longest x16 10.2 us: advance(): new_total = run_total * shrink + jnp.sum(block_expo, axis=-1)]
  transfers between devices with their start and end apart: 4 -> 0, of which waited for: 4 -> 0; matrix products, arithmetic and copies ran while one was open for 12% -> 0% of each run, Pallas kernels for 0% -> 0%
where the time goes in v1:
time: 237 us
  Pallas kernels  235 us (99%)
    pallas_call x1, Pallas kernels, shards(): pl.pallas_call(kernel, out_shape=jax.ShapeDtypeStruct((ROWS, SLICE), BF),...  235 us

profile of v1, /device:TPU:1, one launch (start us, length us, event | category | flops | bytes accessed | tf_op | source)
XLA Modules:
  0.0 236.9 jit_solution(5767210766991996711)
XLA Ops:
  0.0 234.8 %joint_attention.1 = bf16[512,768]{1,0:T(8,128)(2,1)} custom-call(bf16[512,768]{1,0:T(8,128)(2,1)} %img_h.1, f32[3,3072]{1,0:T(4,128)} %mod.1, bf16[3072,384]{1,0:T(8,128)(2,1)} %wq_h.1, bf16[3072,384]{1,0:T(8,128)(2,1)} %wk_h.1, bf16[3072,384]{1,0:T(8,128)(2,1)} %wv_h.1, bf16[384,3072]{1,0:T(8,128)(2,1)} %wo_h.1, f32[1,128]{1,0:T(1,128)} %bitcast.2, ...), custom_call_target="tpu_custom_call" | custom-call | flops 12000000000 | bytes 20000000 | tf_op jit(solution)/shard_map/joint_attention/pallas_call | solution.py:543
  234.8 2.1 copy.14

commit v2 on v1

--- a/solution.py
+++ b/solution.py
@@ -33,8 +33,8 @@
 W_A = KV_FSIB + 8 * PIECES
 W_B = W_A + 3
 W_C = W_B + 3
-W_D = W_C + 3
-O_A = W_D + 1
+W_D = W_C + 12
+O_A = W_D + 3
 O_B = O_A + 4
 O_C = O_B + 3
 O_D = O_C + 3
@@ -71,17 +71,15 @@
     far = {"patch": (1 - zh) * 8 + xx * 2 + cc}
     to_pair = {"tensor": pair}
 
-    def copy(src, dst, i, dev):
+    def copy(src, dst, base, off, dev):
+        i = base + off
         return pltpu.make_async_remote_copy(
             src_ref=src, dst_ref=dst, send_sem=ssem.at[i], recv_sem=rsem.at[i],
             device_id=dev, device_id_type=MESH,
         )
 
-    def got(dst, i):
-        copy(dst, dst, i, sib).wait_recv()
-
-    def sent(src, i):
-        copy(src, src, i, sib).wait_send()
+    def got(dst, base, off=0):
+        copy(dst, dst, base, off, sib).wait_recv()
 
     def block(buf, slot, piece=0, pieces=1):
         n = ROWS // pieces
@@ -102,6 +100,14 @@
         pltpu.make_async_copy(wo_h.at[:, pair_cols], w_o.at[0, :, pl.ds(SLICE, SLICE)], lsem.at[7]),
     ]
 
+    for cp in local:
+        cp.start()
+
+    @pl.when(is_mid)
+    def _():
+        for cp in local_o:
+            cp.start()
+
     peers = [sib, far] + [at_x(d) for d in (1, 2, 3)] + [at_y(d) for d in (1, 2, 3)]
     peers += [{"tensor": lax.rem(t + d, 4)} for d in (1, 2, 3)]
     barrier = pltpu.get_barrier_semaphore()
@@ -115,17 +121,13 @@
     def z_piece(j, p):
         n = ROWS // PIECES
         return copy(
-            stale[j].at[pl.ds(p * n, n)], block(bufs[j], 8, p, PIECES), KV_Z + j * PIECES + p, far
+            stale[j].at[pl.ds(p * n, n)], block(bufs[j], 8, p, PIECES), KV_Z, j * PIECES + p, far
         )
 
-    for p in range(PIECES):
-        for j in range(2):
-            z_piece(j, p).start()
-
     w_rows = pl.ds(pl.multiple_of(cc * 1536 + yy * 384 + xx * 96, 96), 96)
 
     def w_a(j):
-        return copy((wq_h, wk_h, wv_h)[j].at[w_rows], w_end.at[j, w_rows], W_A + j, to_pair)
+        return copy((wq_h, wk_h, wv_h)[j].at[w_rows], w_end.at[j, w_rows], W_A, j, to_pair)
 
     @pl.when(is_end)
     def _():
@@ -135,7 +137,7 @@
     def img_copy(m, c):
         r = lax.rem(t - m + 4, 4)
         rows = pl.ds(pl.multiple_of(c * CH, CH), CH)
-        return copy(img_h.at[rows], img.at[t, rows], IMG + r * NCH + c, {"tensor": jnp.int32(m)})
+        return copy(img_h.at[rows], img.at[t, rows], IMG, r * NCH + c, {"tensor": jnp.int32(m)})
 
     def start_img(c):
         for m in (1, 2):
@@ -143,23 +145,6 @@
             def _(m=m):
                 img_copy(m, c).start()
 
-    for c in range(NCH):
-        start_img(c)
-
-    for j in range(2):
-        copy(stale[j], block(bufs[j], 2), KV_NEAR + 2 * j, at_x(-1)).start()
-        copy(stale[j], block(bufs[j], 4), KV_NEAR + 2 * j + 1, at_x(1)).start()
-    for j in range(2):
-        copy(stale[j], block(bufs[j], 1), KV_SIB + 4 * j, sib).start()
-
-    for cp in local:
-        cp.start()
-
-    @pl.when(is_mid)
-    def _():
-        for cp in local_o:
-            cp.start()
-
     o_rows = pl.ds(pl.multiple_of(cc * 192 + yy * 48, 48), 48)
     o_cols = pl.ds(pl.multiple_of(xx * 384, 384), 384)
 
@@ -168,7 +153,7 @@
         e = 3 * (m - 1)
         start = jnp.where(xx < 2, m, e) * SLICE + lax.rem(xx, 2) * 384
         src = wo_h.at[o_rows, pl.ds(pl.multiple_of(start, 384), 384)]
-        return copy(src, w_o.at[r, o_rows, o_cols], O_A + r, {"tensor": jnp.int32(m)})
+        return copy(src, w_o.at[r, o_rows, o_cols], O_A, r, {"tensor": jnp.int32(m)})
 
     for m in (1, 2):
         @pl.when(t != m)
@@ -180,146 +165,211 @@
 
     def w_b(d):
         piece = w_end.at[:, w_rows]
-        return copy(piece, piece, W_B + d - 1, at_x(d))
-
-    def w_c(d):
-        rows = pl.ds(pl.multiple_of(cc * 1536 + yy * 384, 384), 384)
-        piece = w_end.at[:, rows]
-        return copy(piece, piece, W_C + d - 1, at_y(d))
-
-    def w_d():
-        piece = w_end.at[:, pl.ds(pl.multiple_of(cc * 1536, 1536), 1536)]
-        return copy(piece, piece, W_D, sib)
+        return copy(piece, piece, W_B, d - 1, at_x(d))
+
+    def y_rows(d, half=None):
+        n = 384 if half is None else 192
+        first = cc * 1536 + lax.rem(yy + d + 4, 4) * 384 + (192 if half else 0)
+        return pl.ds(pl.multiple_of(first, n), n)
+
+    def w_c(j, s):
+        piece = w_end.at[j, y_rows(0)]
+        return copy(piece, piece, W_C, 2 * j + s, at_y(1 - 2 * s))
+
+    def w_two(j, s):
+        piece = w_end.at[j, y_rows(2 * s - 1, s)]
+        return copy(piece, piece, W_C, 6 + 2 * j + s, at_y(1 - 2 * s))
+
+    def w_d(j):
+        piece = w_end.at[j, pl.ds(pl.multiple_of(cc * 1536, 1536), 1536)]
+        return copy(piece, piece, W_D, j, sib)
+
+    def w_forward(j):
+        for s in (0, 1):
+            got(w_end.at[j, y_rows(2 * s - 1)], W_C, 2 * j + s)
+            w_two(j, s).start()
+
+    def w_share(j):
+        for s in (0, 1):
+            got(w_end.at[j, y_rows(2, s)], W_C, 6 + 2 * j + s)
+        w_d(j).start()
 
     def o_b(d):
         piece = w_o.at[pl.ds(1, 3), o_rows, o_cols]
-        return copy(piece, piece, O_B + d - 1, at_x(d))
+        return copy(piece, piece, O_B, d - 1, at_x(d))
 
     def o_c(d):
         piece = w_o.at[pl.ds(1, 3), o_rows]
-        return copy(piece, piece, O_C + d - 1, at_y(d))
+        return copy(piece, piece, O_C, d - 1, at_y(d))
 
     def o_d():
         piece = w_o.at[pl.ds(1, 3), pl.ds(pl.multiple_of(cc * 192, 192), 192)]
-        return copy(piece, piece, O_D, sib)
+        return copy(piece, piece, O_D, 0, sib)
 
     def wait_w_b():
         for d in (1, 2, 3):
             rows = pl.ds(pl.multiple_of(cc * 1536 + yy * 384 + lax.rem(xx - d + 4, 4) * 96, 96), 96)
-            got(w_end.at[:, rows], W_B + d - 1)
-
-    def wait_w_c():
-        for d in (1, 2, 3):
-            rows = pl.ds(pl.multiple_of(cc * 1536 + lax.rem(yy - d + 4, 4) * 384, 384), 384)
-            got(w_end.at[:, rows], W_C + d - 1)
+            got(w_end.at[:, rows], W_B, d - 1)
 
     def wait_o_b():
         for d in (1, 2, 3):
             cols = pl.ds(pl.multiple_of(lax.rem(xx - d + 4, 4) * 384, 384), 384)
-            got(w_o.at[pl.ds(1, 3), o_rows, cols], O_B + d - 1)
+            got(w_o.at[pl.ds(1, 3), o_rows, cols], O_B, d - 1)
 
     def wait_o_c():
         for d in (1, 2, 3):
             rows = pl.ds(pl.multiple_of(cc * 192 + lax.rem(yy - d + 4, 4) * 48, 48), 48)
-            got(w_o.at[pl.ds(1, 3), rows], O_C + d - 1)
-
-    @pl.when(is_mid)
-    def _():
-        for j in range(3):
-            got(w_end.at[j, w_rows], W_A + j)
-        for d in (1, 2, 3):
-            w_b(d).start()
-        for r in (1, 2, 3):
-            got(w_o.at[r, o_rows, o_cols], O_A + r)
-        for d in (1, 2, 3):
-            o_b(d).start()
+            got(w_o.at[pl.ds(1, 3), rows], O_C, d - 1)
 
     def near_sib(j, i):
         src = stale[j] if i == 0 else block(bufs[j], 2 * i)
-        return copy(src, block(bufs[j], 2 * i + 1), KV_SIB + 4 * j + i, sib)
+        return copy(src, block(bufs[j], 2 * i + 1), KV_SIB, 4 * j + i, sib)
 
     def near_two(j):
         if j == 0:
-            return copy(block(kbuf, 4), block(kbuf, 6), KV_TWO, at_x(1))
-        return copy(block(vbuf, 2), block(vbuf, 6), KV_TWO + 1, at_x(-1))
-
-    @pl.when(is_mid)
-    def _():
-        wait_w_b()
-        for d in (1, 2, 3):
-            w_c(d).start()
-        wait_o_b()
-        for d in (1, 2, 3):
-            o_c(d).start()
-
-    got(block(kbuf, 4), KV_NEAR + 1)
-    near_two(0).start()
-    got(block(vbuf, 2), KV_NEAR + 2)
-    near_two(1).start()
-    near_sib(0, 2).start()
-    near_sib(1, 1).start()
-    got(block(kbuf, 2), KV_NEAR)
-    near_sib(0, 1).start()
-    got(block(vbuf, 4), KV_NEAR + 3)
-    near_sib(1, 2).start()
-
-    @pl.when(is_mid)
-    def _():
-        wait_w_c()
-        w_d().start()
-        wait_o_c()
-        o_d().start()
+            return copy(block(kbuf, 4), block(kbuf, 6), KV_TWO, 0, at_x(1))
+        return copy(block(vbuf, 2), block(vbuf, 6), KV_TWO, 1, at_x(-1))
 
     def far_x(j, p, s):
         src = block(bufs[j], 8, p, PIECES)
         dst = block(bufs[j], 10 + 2 * s, p, PIECES)
-        return copy(src, dst, KV_FX + (j * PIECES + p) * 2 + s, at_x(-1 if s == 0 else 1))
+        return copy(src, dst, KV_FX, (j * PIECES + p) * 2 + s, at_x(-1 if s == 0 else 1))
 
     def far_two(j, p):
         src = block(bufs[j], 12 if j == 0 else 10, p, PIECES)
         dst = block(bufs[j], 14, p, PIECES)
-        return copy(src, dst, KV_FTWO + j * PIECES + p, at_x(1 if j == 0 else -1))
+        return copy(src, dst, KV_FTWO, j * PIECES + p, at_x(1 if j == 0 else -1))
 
     def far_sib(j, p, i):
         src = block(bufs[j], 8 + 2 * i, p, PIECES)
         dst = block(bufs[j], 9 + 2 * i, p, PIECES)
-        return copy(src, dst, KV_FSIB + (j * PIECES + p) * 4 + i, sib)
-
-    for p in range(PIECES):
+        return copy(src, dst, KV_FSIB, (j * PIECES + p) * 4 + i, sib)
+
+    def far_z(j, p):
+        got(block(bufs[j], 8, p, PIECES), KV_Z, j * PIECES + p)
+        far_x(j, p, 0).start()
+        far_x(j, p, 1).start()
+        far_sib(j, p, 0).start()
+
+    def far_on(p):
         for j in range(2):
-            got(block(bufs[j], 8, p, PIECES), KV_Z + j * PIECES + p)
-            far_x(j, p, 0).start()
-            far_x(j, p, 1).start()
-            far_sib(j, p, 0).start()
-
-    for j in range(2):
-        got(block(bufs[j], 6), KV_TWO + j)
-        near_sib(j, 3).start()
-
-    def far_rest():
+            for s in (0, 1):
+                got(block(bufs[j], 10 + 2 * s, p, PIECES), KV_FX, (j * PIECES + p) * 2 + s)
+            far_two(j, p).start()
+            far_sib(j, p, 1).start()
+            far_sib(j, p, 2).start()
+
+    def far_last():
         for p in range(PIECES):
             for j in range(2):
-                for s in (0, 1):
-                    got(block(bufs[j], 10 + 2 * s, p, PIECES), KV_FX + (j * PIECES + p) * 2 + s)
-                far_two(j, p).start()
-                far_sib(j, p, 1).start()
-                far_sib(j, p, 2).start()
-        for p in range(PIECES):
-            for j in range(2):
-                got(block(bufs[j], 14, p, PIECES), KV_FTWO + j * PIECES + p)
+                got(block(bufs[j], 14, p, PIECES), KV_FTWO, j * PIECES + p)
                 far_sib(j, p, 3).start()
+
+    def far_rest():
         for p in range(PIECES):
             for j in range(2):
                 for i in range(4):
                     got(
                         block(bufs[j], 9 + 2 * i, p, PIECES),
-                        KV_FSIB + (j * PIECES + p) * 4 + i,
+                        KV_FSIB, (j * PIECES + p) * 4 + i,
                     )
+
+    def near_on():
+        got(block(kbuf, 4), KV_NEAR, 1)
+        near_two(0).start()
+        got(block(vbuf, 2), KV_NEAR, 2)
+        near_two(1).start()
+        near_sib(0, 2).start()
+        near_sib(1, 1).start()
+        got(block(kbuf, 2), KV_NEAR)
+        near_sib(0, 1).start()
+        got(block(vbuf, 4), KV_NEAR, 3)
+        near_sib(1, 2).start()
+
+    def near_last():
+        for j in range(2):
+            got(block(bufs[j], 6), KV_TWO, j)
+            near_sib(j, 3).start()
+
+    def start_near():
+        for j in range(2):
+            copy(stale[j], block(bufs[j], 2), KV_NEAR, 2 * j, at_x(-1)).start()
+            copy(stale[j], block(bufs[j], 4), KV_NEAR, 2 * j + 1, at_x(1)).start()
+
+    for j in range(2):
+        copy(stale[j], block(bufs[j], 1), KV_SIB, 4 * j, sib).start()
+
+    @pl.when(is_end)
+    def _():
+        start_near()
+        for j in range(3):
+            w_a(j).wait_send()
+
+    @pl.when(is_mid)
+    def _():
+        for j in range(3):
+            got(w_end.at[j, w_rows], W_A, j)
+        for d in (1, 2, 3):
+            w_b(d).start()
+
+    for m in (1, 2):
+        @pl.when(t != m)
+        def _(m=m):
+            o_a(m).wait_send()
+
+    @pl.when(is_mid)
+    def _():
+        for r in (1, 2, 3):
+            got(w_o.at[r, o_rows, o_cols], O_A, r)
+
+    for p in range(PIECES):
+        for j in range(2):
+            z_piece(j, p).start()
+
+    for c in range(NCH):
+        start_img(c)
+
+    @pl.when(is_end)
+    def _():
+        far_z(0, 0)
+        far_z(1, 0)
+        near_on()
+        far_z(0, 1)
+        far_z(1, 1)
+        far_on(0)
+        near_last()
+        far_on(1)
+        far_last()
+
+    @pl.when(is_mid)
+    def _():
+        wait_w_b()
+        for j in range(3):
+            for s in (0, 1):
+                w_c(j, s).start()
+        start_near()
+        for d in (1, 2, 3):
+            o_b(d).start()
+        far_z(0, 0)
+        w_forward(0)
+        far_z(1, 0)
+        w_forward(1)
+        far_z(0, 1)
+        far_z(1, 1)
+        w_forward(2)
+        near_on()
+        far_on(0)
+        wait_o_b()
+        for d in (1, 2, 3):
+            o_c(d).start()
+        for j in range(3):
+            w_share(j)
+        near_last()
 
     def near_rest():
         for j in range(2):
             for i in range(4):
-                got(block(bufs[j], 2 * i + 1), KV_SIB + 4 * j + i)
+                got(block(bufs[j], 2 * i + 1), KV_SIB, 4 * j + i)
 
     def chunk_rows(c, base=0):
         return pl.ds(pl.multiple_of(base + c * CH, CH), CH)
@@ -362,35 +412,41 @@
             kbuf.at[chunk_rows(c, FRESH)],
             vbuf.at[chunk_rows(c, FRESH)],
         )[j]
-        return copy(stage.at[j, chunk_rows(c)], dst, QKV + j * NCH + c, to_pair)
+        return copy(stage.at[j, chunk_rows(c)], dst, QKV, j * NCH + c, to_pair)
+
+    def middle_chunk(c):
+        for r in (1, 2, 3):
+            s = lax.rem(t + r, 4)
+            got(img.at[s, chunk_rows(c)], IMG, r * NCH + c)
+        norm_chunk(c)
+
+        def put_end(j, v):
+            stage[j, chunk_rows(c)] = v
+            qkv_copy(j, c).start()
+
+        project(w_end, put_end)
+
+        def put_own(j, v):
+            if j == 0:
+                qbuf[chunk_rows(c)] = v
+            else:
+                bufs[j - 1][chunk_rows(c, FRESH)] = v
+
+        project(w_own, put_own)
+
+    def end_chunk(c):
+        got(qbuf.at[chunk_rows(c)], QKV, c)
+        got(kbuf.at[chunk_rows(c, FRESH)], QKV, NCH + c)
+        got(vbuf.at[chunk_rows(c, FRESH)], QKV, 2 * NCH + c)
 
     def fresh_chunk(c):
         @pl.when(is_mid)
         def _():
-            for r in (1, 2, 3):
-                s = lax.rem(t + r, 4)
-                got(img.at[s, chunk_rows(c)], IMG + r * NCH + c)
-            norm_chunk(c)
-
-            def put_end(j, v):
-                stage[j, chunk_rows(c)] = v
-                qkv_copy(j, c).start()
-
-            project(w_end, put_end)
-
-            def put_own(j, v):
-                if j == 0:
-                    qbuf[chunk_rows(c)] = v
-                else:
-                    bufs[j - 1][chunk_rows(c, FRESH)] = v
-
-            project(w_own, put_own)
+            middle_chunk(c)
 
         @pl.when(is_end)
         def _():
-            got(qbuf.at[chunk_rows(c)], QKV + c)
-            got(kbuf.at[chunk_rows(c, FRESH)], QKV + NCH + c)
-            got(vbuf.at[chunk_rows(c, FRESH)], QKV + 2 * NCH + c)
+            end_chunk(c)
 
     def attend(c, start, n):
         rows = chunk_rows(c)
@@ -414,7 +470,7 @@
     def tail_copy(m, c):
         r = lax.rem(t - m + 4, 4)
         rows = chunk_rows(c)
-        return copy(att.at[0, rows], att.at[r, rows], TAIL + r * NCH + c, {"tensor": jnp.int32(m)})
+        return copy(att.at[0, rows], att.at[r, rows], TAIL, r * NCH + c, {"tensor": jnp.int32(m)})
 
     def finish(c):
         attend(c, FRESH, ROWS)
@@ -434,10 +490,21 @@
     def _():
         for cp in local_o:
             cp.wait()
-        got(w_end.at[:, pl.ds(pl.multiple_of((1 - cc) * 1536, 1536), 1536)], W_D)
-        got(w_o.at[pl.ds(1, 3), pl.ds(pl.multiple_of((1 - cc) * 192, 192), 192)], O_D)
-
-    @pl.loop(0, NCH)
+        for j in range(3):
+            rows = pl.ds(pl.multiple_of((1 - cc) * 1536, 1536), 1536)
+            got(w_end.at[j, rows], W_D, j)
+
+    def near(c):
+        @pl.loop(0, 4096 // KB)
+        def _(b):
+            attend(c, b * KB, KB)
+
+    def distant(c):
+        @pl.loop(4096 // KB, 8192 // KB)
+        def _(b):
+            attend(c, b * KB, KB)
+
+    @pl.loop(0, NCH - 1)
     def _(c):
         fresh_chunk(c)
 
@@ -445,28 +512,50 @@
         def _():
             near_rest()
 
-        @pl.when(c == NCH - 1)
+        near(c)
+        @pl.when((c == 0) & is_mid)
         def _():
-            @pl.loop(0, NCH - 1)
-            def _(d):
-                finish(d)
-
-        @pl.loop(0, 4096 // KB)
-        def _(b):
-            attend(c, b * KB, KB)
-
-        @pl.when(c == 0)
+            far_on(1)
+
+        @pl.when((c == 1) & is_mid)
         def _():
-            far_rest()
-
-        @pl.loop(4096 // KB, 8192 // KB)
-        def _(b):
-            attend(c, b * KB, KB)
+            far_last()
+
+        @pl.when((c == NCH - 2) & is_mid)
+        def _():
+            wait_o_c()
+            o_d().start()
+
+    @pl.when(is_mid)
+    def _():
+        middle_chunk(NCH - 1)
+
+    far_rest()
+
+    @pl.loop(0, NCH - 1)
+    def _(c):
+        distant(c)
+
+    @pl.when(is_end)
+    def _():
+        end_chunk(NCH - 1)
+
+    @pl.loop(0, NCH - 1)
+    def _(c):
+        finish(c)
+
+    @pl.loop(0, 8192 // KB)
+    def _(b):
+        attend(NCH - 1, b * KB, KB)
 
     finish(NCH - 1)
 
+    @pl.when(is_mid)
+    def _():
+        got(w_o.at[pl.ds(1, 3), pl.ds(pl.multiple_of((1 - cc) * 192, 192), 192)], O_D)
+
     def out_copy(c):
-        return copy(ostage.at[chunk_rows(c)], out.at[chunk_rows(c)], OUT + c, to_pair)
+        return copy(ostage.at[chunk_rows(c)], out.at[chunk_rows(c)], OUT, c, to_pair)
 
     @pl.when(is_mid)
     def _():
@@ -477,7 +566,7 @@
         def _(c):
             rows = chunk_rows(c)
             for r in (1, 2, 3):
-                got(att.at[r, rows], TAIL + r * NCH + c)
+                got(att.at[r, rows], TAIL, r * NCH + c)
             for half, gate in ((1, gate_end), (0, gate_own)):
                 y = jnp.zeros((CH, SLICE), F32)
                 for r in range(4):
@@ -493,7 +582,7 @@
     @pl.when(is_end)
     def _():
         for c in range(NCH):
-            got(out.at[chunk_rows(c)], OUT + c)
+            got(out.at[chunk_rows(c)], OUT, c)
 
     for j in range(2):
         for p in range(PIECES):
@@ -504,20 +593,14 @@
             for i in range(4):
                 far_sib(j, p, i).wait_send()
         for s in range(2):
-            sent(stale[j], KV_NEAR + 2 * j + s)
+            copy(stale[j], block(bufs[j], 2), KV_NEAR, 2 * j + s, at_x(1)).wait_send()
         for i in range(4):
             near_sib(j, i).wait_send()
         near_two(j).wait_send()
 
-    @pl.when(is_end)
-    def _():
-        for j in range(3):
-            w_a(j).wait_send()
-
     for m in (1, 2):
         @pl.when(t != m)
         def _(m=m):
-            o_a(m).wait_send()
             for c in range(NCH):
                 img_copy(m, c).wait_send()
                 tail_copy(m, c).wait_send()
@@ -526,10 +609,13 @@
     def _():
         for d in (1, 2, 3):
             w_b(d).wait_send()
-            w_c(d).wait_send()
             o_b(d).wait_send()
             o_c(d).wait_send()
-        w_d().wait_send()
+        for j in range(3):
+            w_d(j).wait_send()
+            for s in (0, 1):
+                w_c(j, s).wait_send()
+                w_two(j, s).wait_send()
         o_d().wait_send()
         for c in range(NCH):
             out_copy(c).wait_send()

time: 237 us -> 143 us (0.60)
  Pallas kernels: 235 us -> 140 us
    pallas_call x1, Pallas kernels: 235 us -> 140 us  [shards(): pl.pallas_call(kernel, out_shape=jax.ShapeDtypeStruct((ROWS, SLICE), BF),...]
where the time goes in v2:
time: 143 us; the launch traced here: 142 us
  Pallas kernels  140 us (98%)
  local copies, waits for them, and re-layouts  2.06 us (1%)
    pallas_call x1, Pallas kernels, shards(): pl.pallas_call(kernel, out_shape=jax.ShapeDtypeStruct((ROWS, SLICE), BF),...  140 us

profile of v2, /device:TPU:1, one launch (start us, length us, event | category | flops | bytes accessed | tf_op | source)
XLA Modules:
  0.0 141.6 jit_solution(11145248001399926145)
XLA Ops:
  0.0 139.5 %joint_attention.1 = bf16[512,768]{1,0:T(8,128)(2,1)} custom-call(bf16[512,768]{1,0:T(8,128)(2,1)} %img_h.1, f32[3,3072]{1,0:T(4,128)} %mod.1, bf16[3072,384]{1,0:T(8,128)(2,1)} %wq_h.1, bf16[3072,384]{1,0:T(8,128)(2,1)} %wk_h.1, bf16[3072,384]{1,0:T(8,128)(2,1)} %wv_h.1, bf16[384,3072]{1,0:T(8,128)(2,1)} %wo_h.1, f32[1,128]{1,0:T(1,128)} %bitcast.2, ...), custom_call_target="tpu_custom_call" | custom-call | flops 12000000000 | bytes 20000000 | tf_op jit(solution)/shard_map/joint_attention/pallas_call | solution.py:629
  139.5 2.1 %copy.14 = bf16[512,768]{1,0:T(8,128)(2,1)} copy(bf16[512,768]{1,0:T(8,128)(2,1)} %joint_attention.1) | data formatting | bytes 1572864

commit v3 on v2

--- a/solution.py
+++ b/solution.py
@@ -32,7 +32,7 @@
 KV_FSIB = KV_FTWO + 2 * PIECES
 W_A = KV_FSIB + 8 * PIECES
 W_B = W_A + 3
-W_C = W_B + 3
+W_C = W_B + 9
 W_D = W_C + 12
 O_A = W_D + 3
 O_B = O_A + 4
@@ -163,9 +163,9 @@
     m_s[...] = jnp.full(m_s.shape, -1e30, F32)
     acc_s[...] = jnp.zeros(acc_s.shape, F32)
 
-    def w_b(d):
-        piece = w_end.at[:, w_rows]
-        return copy(piece, piece, W_B, d - 1, at_x(d))
+    def w_b(j, d):
+        piece = w_end.at[j, w_rows]
+        return copy(piece, piece, W_B, 3 * j + d - 1, at_x(d))
 
     def y_rows(d, half=None):
         n = 384 if half is None else 192
@@ -206,10 +206,10 @@
         piece = w_o.at[pl.ds(1, 3), pl.ds(pl.multiple_of(cc * 192, 192), 192)]
         return copy(piece, piece, O_D, 0, sib)
 
-    def wait_w_b():
+    def wait_w_b(j):
         for d in (1, 2, 3):
             rows = pl.ds(pl.multiple_of(cc * 1536 + yy * 384 + lax.rem(xx - d + 4, 4) * 96, 96), 96)
-            got(w_end.at[:, rows], W_B, d - 1)
+            got(w_end.at[j, rows], W_B, 3 * j + d - 1)
 
     def wait_o_b():
         for d in (1, 2, 3):
@@ -309,8 +309,8 @@
     def _():
         for j in range(3):
             got(w_end.at[j, w_rows], W_A, j)
-        for d in (1, 2, 3):
-            w_b(d).start()
+            for d in (1, 2, 3):
+                w_b(j, d).start()
 
     for m in (1, 2):
         @pl.when(t != m)
@@ -328,48 +328,6 @@
 
     for c in range(NCH):
         start_img(c)
-
-    @pl.when(is_end)
-    def _():
-        far_z(0, 0)
-        far_z(1, 0)
-        near_on()
-        far_z(0, 1)
-        far_z(1, 1)
-        far_on(0)
-        near_last()
-        far_on(1)
-        far_last()
-
-    @pl.when(is_mid)
-    def _():
-        wait_w_b()
-        for j in range(3):
-            for s in (0, 1):
-                w_c(j, s).start()
-        start_near()
-        for d in (1, 2, 3):
-            o_b(d).start()
-        far_z(0, 0)
-        w_forward(0)
-        far_z(1, 0)
-        w_forward(1)
-        far_z(0, 1)
-        far_z(1, 1)
-        w_forward(2)
-        near_on()
-        far_on(0)
-        wait_o_b()
-        for d in (1, 2, 3):
-            o_c(d).start()
-        for j in range(3):
-            w_share(j)
-        near_last()
-
-    def near_rest():
-        for j in range(2):
-            for i in range(4):
-                got(block(bufs[j], 2 * i + 1), KV_SIB, 4 * j + i)
 
     def chunk_rows(c, base=0):
         return pl.ds(pl.multiple_of(base + c * CH, CH), CH)
@@ -388,13 +346,13 @@
         for s in range(4):
             cols = slice(s * SLICE, (s + 1) * SLICE)
             d = (img[s, rows].astype(F32) - mean) * rstd
-            modl[:, cols] = (d * (1.0 + mod[1:2, cols]) + mod[0:1, cols]).astype(BF)
-
-    def project(w, put):
-        for j in range(3):
-            y = jnp.dot(modl[...], w[j], preferred_element_type=F32)
+            modl[rows, cols] = (d * (1.0 + mod[1:2, cols]) + mod[0:1, cols]).astype(BF)
+
+    def project(c, w, put):
+        for j in (1, 2, 0):
+            y = jnp.dot(modl[chunk_rows(c)], w[j], preferred_element_type=F32)
             if j == 2:
-                put(j, y.astype(BF))
+                put(c, j, y.astype(BF))
                 continue
             gain = qgain[...] * (LOG2E / math.sqrt(HW)) if j == 0 else kgain[...]
             parts = []
@@ -402,7 +360,7 @@
                 v = y[:, h * HW : (h + 1) * HW]
                 power = jnp.mean(v * v, axis=1, keepdims=True)
                 parts.append((v * lax.rsqrt(power + 1e-06) * gain).astype(BF))
-            put(j, jnp.concatenate(parts, axis=1))
+            put(c, j, jnp.concatenate(parts, axis=1))
 
     FRESH = 16 * ROWS
 
@@ -414,31 +372,40 @@
         )[j]
         return copy(stage.at[j, chunk_rows(c)], dst, QKV, j * NCH + c, to_pair)
 
-    def middle_chunk(c):
+    def image_chunk(c):
         for r in (1, 2, 3):
             s = lax.rem(t + r, 4)
             got(img.at[s, chunk_rows(c)], IMG, r * NCH + c)
         norm_chunk(c)
 
-        def put_end(j, v):
-            stage[j, chunk_rows(c)] = v
-            qkv_copy(j, c).start()
-
-        project(w_end, put_end)
-
-        def put_own(j, v):
-            if j == 0:
-                qbuf[chunk_rows(c)] = v
-            else:
-                bufs[j - 1][chunk_rows(c, FRESH)] = v
-
-        project(w_own, put_own)
-
-    def end_chunk(c):
-        got(qbuf.at[chunk_rows(c)], QKV, c)
+    def put_end(c, j, v):
+        stage[j, chunk_rows(c)] = v
+        qkv_copy(j, c).start()
+
+    def put_own(c, j, v):
+        if j == 0:
+            qbuf[chunk_rows(c)] = v
+        else:
+            bufs[j - 1][chunk_rows(c, FRESH)] = v
+
+    def middle_chunk(c):
+        @pl.when(c > 0)
+        def _():
+            image_chunk(c)
+
+        project(c, w_end, put_end)
+
+        @pl.when(c > 0)
+        def _():
+            project(c, w_own, put_own)
+
+    def end_fresh(c):
         got(kbuf.at[chunk_rows(c, FRESH)], QKV, NCH + c)
         got(vbuf.at[chunk_rows(c, FRESH)], QKV, 2 * NCH + c)
 
+    def end_query(c):
+        got(qbuf.at[chunk_rows(c)], QKV, c)
+
     def fresh_chunk(c):
         @pl.when(is_mid)
         def _():
@@ -446,7 +413,56 @@
 
         @pl.when(is_end)
         def _():
-            end_chunk(c)
+            end_fresh(c)
+            end_query(c)
+
+    for cp in local:
+        cp.wait()
+
+    @pl.when(is_end)
+    def _():
+        far_z(0, 0)
+        far_z(1, 0)
+        near_on()
+        far_z(0, 1)
+        far_z(1, 1)
+        far_on(0)
+        near_last()
+        far_on(1)
+        far_last()
+
+    @pl.when(is_mid)
+    def _():
+        for j in range(3):
+            wait_w_b(j)
+            for s in (0, 1):
+                w_c(j, s).start()
+        start_near()
+        for d in (1, 2, 3):
+            o_b(d).start()
+        w_forward(0)
+        w_forward(1)
+        far_z(0, 0)
+        far_z(1, 0)
+        w_forward(2)
+        near_on()
+        w_share(0)
+        far_z(0, 1)
+        w_share(1)
+        far_z(1, 1)
+        w_share(2)
+        wait_o_b()
+        for d in (1, 2, 3):
+            o_c(d).start()
+        far_on(0)
+        near_last()
+        image_chunk(0)
+        project(0, w_own, put_own)
+
+    def near_rest():
+        for j in range(2):
+            for i in range(4):
+                got(block(bufs[j], 2 * i + 1), KV_SIB, 4 * j + i)
 
     def attend(c, start, n):
         rows = chunk_rows(c)
@@ -467,10 +483,22 @@
             pv = jnp.dot(p, both, preferred_element_type=F32)
             acc_s[h, rows] = acc_s[h, rows] * jnp.concatenate([shrink, shrink], axis=1) + pv
 
-    def tail_copy(m, c):
-        r = lax.rem(t - m + 4, 4)
+    other = jnp.where(is_mid, 3 - t, pair)
+    from_end = lax.rem(pair - t + 4, 4)
+
+    def tail_copy(c):
         rows = chunk_rows(c)
-        return copy(att.at[0, rows], att.at[r, rows], TAIL, r * NCH + c, {"tensor": jnp.int32(m)})
+        r = lax.rem(t - other + 4, 4)
+        return copy(att.at[0, rows], att.at[r, rows], TAIL, r * NCH + c, {"tensor": other})
+
+    def relay_copy(c):
+        rows = chunk_rows(c)
+        src = att.at[from_end, rows]
+        return copy(src, att.at[2, rows], TAIL, 2 * NCH + c, {"tensor": other})
+
+    def relay(c):
+        got(att.at[from_end, chunk_rows(c)], TAIL, from_end * NCH + c)
+        relay_copy(c).start()
 
     def finish(c):
         attend(c, FRESH, ROWS)
@@ -478,13 +506,27 @@
         for h in range(HEADS):
             a = acc_s[h, rows]
             att[0, rows, h * HW : (h + 1) * HW] = (a[:, :HW] / a[:, HW:]).astype(BF)
-        for m in (1, 2):
-            @pl.when(t != m)
-            def _(m=m):
-                tail_copy(m, c).start()
-
-    for cp in local:
-        cp.wait()
+        tail_copy(c).start()
+
+    def out_copy(c):
+        return copy(ostage.at[chunk_rows(c)], out.at[chunk_rows(c)], OUT, c, to_pair)
+
+    def project_out(c):
+        rows = chunk_rows(c)
+        r = 4 - from_end
+        got(att.at[r, rows], TAIL, r * NCH + c)
+        got(att.at[2, rows], TAIL, 2 * NCH + c)
+        for half, cols in ((1, pair_cols), (0, my_cols)):
+            y = jnp.zeros((CH, SLICE), F32)
+            for r in range(4):
+                w = w_o[r, :, half * SLICE : (half + 1) * SLICE]
+                y += jnp.dot(att[r, rows], w, preferred_element_type=F32)
+            y = (y * mod[2:3, cols]).astype(BF)
+            if half:
+                ostage[rows] = y
+                out_copy(c).start()
+            else:
+                out[rows] = y
 
     @pl.when(is_mid)
     def _():
@@ -513,71 +555,67 @@
             near_rest()
 
         near(c)
+
         @pl.when((c == 0) & is_mid)
         def _():
             far_on(1)
 
-        @pl.when((c == 1) & is_mid)
-        def _():
-            far_last()
-
-        @pl.when((c == NCH - 2) & is_mid)
-        def _():
-            wait_o_c()
-            o_d().start()
+        @pl.when(c == 1)
+        def _():
+            @pl.when(is_mid)
+            def _():
+                far_last()
+
+            far_rest()
+
+        @pl.when(c > 0)
+        def _():
+            distant(c - 1)
 
     @pl.when(is_mid)
     def _():
+        wait_o_c()
+        o_d().start()
         middle_chunk(NCH - 1)
 
-    far_rest()
-
-    @pl.loop(0, NCH - 1)
-    def _(c):
-        distant(c)
+    distant(NCH - 2)
 
     @pl.when(is_end)
     def _():
-        end_chunk(NCH - 1)
+        end_fresh(NCH - 1)
 
     @pl.loop(0, NCH - 1)
     def _(c):
         finish(c)
 
+    @pl.when(is_end)
+    def _():
+        end_query(NCH - 1)
+
     @pl.loop(0, 8192 // KB)
     def _(b):
         attend(NCH - 1, b * KB, KB)
 
+        @pl.when((b > 0) & is_mid)
+        def _():
+            relay(b - 1)
+
+            @pl.when(b == 8192 // KB - 1)
+            def _():
+                got(w_o.at[pl.ds(1, 3), pl.ds(pl.multiple_of((1 - cc) * 192, 192), 192)], O_D)
+                project_out(0)
+
     finish(NCH - 1)
 
     @pl.when(is_mid)
     def _():
-        got(w_o.at[pl.ds(1, 3), pl.ds(pl.multiple_of((1 - cc) * 192, 192), 192)], O_D)
-
-    def out_copy(c):
-        return copy(ostage.at[chunk_rows(c)], out.at[chunk_rows(c)], OUT, c, to_pair)
-
-    @pl.when(is_mid)
-    def _():
-        gate_own = mod[2:3, my_cols]
-        gate_end = mod[2:3, pair_cols]
-
-        @pl.loop(0, NCH)
+        @pl.loop(1, NCH)
         def _(c):
-            rows = chunk_rows(c)
-            for r in (1, 2, 3):
-                got(att.at[r, rows], TAIL, r * NCH + c)
-            for half, gate in ((1, gate_end), (0, gate_own)):
-                y = jnp.zeros((CH, SLICE), F32)
-                for r in range(4):
-                    w = w_o[r, :, half * SLICE : (half + 1) * SLICE]
-                    y += jnp.dot(att[r, rows], w, preferred_element_type=F32)
-                y = (y * gate).astype(BF)
-                if half:
-                    ostage[rows] = y
-                    out_copy(c).start()
-                else:
-                    out[rows] = y
+            @pl.when(c == 2)
+            def _():
+                relay(NCH - 1)
+
+            project_out(c)
 
     @pl.when(is_end)
     def _():
@@ -603,12 +641,15 @@
         def _(m=m):
             for c in range(NCH):
                 img_copy(m, c).wait_send()
-                tail_copy(m, c).wait_send()
+
+    for c in range(NCH):
+        tail_copy(c).wait_send()
 
     @pl.when(is_mid)
     def _():
         for d in (1, 2, 3):
-            w_b(d).wait_send()
+            for j in range(3):
+                w_b(j, d).wait_send()
             o_b(d).wait_send()
             o_c(d).wait_send()
         for j in range(3):
@@ -619,6 +660,7 @@
         o_d().wait_send()
         for c in range(NCH):
             out_copy(c).wait_send()
+            relay_copy(c).wait_send()
             for j in range(3):
                 qkv_copy(j, c).wait_send()
 
@@ -638,7 +680,7 @@
             pltpu.VMEM((3, DM, WIDE), BF),
             pltpu.VMEM((3, DM, WIDE), BF),
             pltpu.VMEM((4, WIDE, 2 * SLICE), BF),
-            pltpu.VMEM((CH, DM), BF),
+            pltpu.VMEM((ROWS, DM), BF),
             pltpu.VMEM((ROWS, WIDE), BF),
             pltpu.VMEM((3, ROWS, WIDE), BF),
             pltpu.VMEM((4, ROWS, WIDE), BF),

time: 143 us -> 137 us (0.958)
  Pallas kernels: 140 us -> 134 us
    pallas_call x1, Pallas kernels: 140 us -> 134 us  [shards(): pl.pallas_call(kernel, out_shape=jax.ShapeDtypeStruct((ROWS, SLICE), BF),...]
where the time goes in v3:
time: 137 us
  Pallas kernels  134 us (98%)
  local copies, waits for them, and re-layouts  2.06 us (2%)
    pallas_call x1, Pallas kernels, shards(): pl.pallas_call(kernel, out_shape=jax.ShapeDtypeStruct((ROWS, SLICE), BF),...  134 us

profile of v3, /device:TPU:1, one launch (start us, length us, event | category | flops | bytes accessed | tf_op | source)
XLA Modules:
  0.0 136.5 jit_solution(11622318424425538158)
XLA Ops:
  0.0 134.5 %joint_attention.1 = bf16[512,768]{1,0:T(8,128)(2,1)} custom-call(bf16[512,768]{1,0:T(8,128)(2,1)} %img_h.1, f32[3,3072]{1,0:T(4,128)} %mod.1, bf16[3072,384]{1,0:T(8,128)(2,1)} %wq_h.1, bf16[3072,384]{1,0:T(8,128)(2,1)} %wk_h.1, bf16[3072,384]{1,0:T(8,128)(2,1)} %wv_h.1, bf16[384,3072]{1,0:T(8,128)(2,1)} %wo_h.1, f32[1,128]{1,0:T(1,128)} %bitcast.2, ...), custom_call_target="tpu_custom_call" | custom-call | flops 12000000000 | bytes 20000000 | tf_op jit(solution)/shard_map/joint_attention/pallas_call | solution.py:671
  134.5 2.1 %copy.14 = bf16[512,768]{1,0:T(8,128)(2,1)} copy(bf16[512,768]{1,0:T(8,128)(2,1)} %joint_attention.1) | data formatting | bytes 1572864

commit v4 on v3

--- a/solution.py
+++ b/solution.py
@@ -556,40 +556,43 @@
 
         near(c)
 
-        @pl.when((c == 0) & is_mid)
+        @pl.when((c == 1) & is_mid)
         def _():
             far_on(1)
 
-        @pl.when(c == 1)
-        def _():
-            @pl.when(is_mid)
-            def _():
-                far_last()
-
+        @pl.when((c == 2) & is_mid)
+        def _():
+            far_last()
+
+        @pl.when((c == 1) & is_end)
+        def _():
             far_rest()
 
-        @pl.when(c > 0)
+        @pl.when((c > 0) & is_end)
         def _():
             distant(c - 1)
 
     @pl.when(is_mid)
     def _():
+        middle_chunk(NCH - 1)
         wait_o_c()
         o_d().start()
-        middle_chunk(NCH - 1)
-
-    distant(NCH - 2)
+        far_rest()
+
+        @pl.loop(0, NCH - 1)
+        def _(c):
+            distant(c)
+            finish(c)
 
     @pl.when(is_end)
     def _():
+        distant(NCH - 2)
         end_fresh(NCH - 1)
 
-    @pl.loop(0, NCH - 1)
-    def _(c):
-        finish(c)
-
-    @pl.when(is_end)
-    def _():
+        @pl.loop(0, NCH - 1)
+        def _(c):
+            finish(c)
+
         end_query(NCH - 1)
 
     @pl.loop(0, 8192 // KB)

time: 137 us -> 132 us (0.964)
  Pallas kernels: 134 us -> 129 us
    pallas_call x1, Pallas kernels: 134 us -> 129 us  [shards(): pl.pallas_call(kernel, out_shape=jax.ShapeDtypeStruct((ROWS, SLICE), BF),...]
where the time goes in v4:
time: 132 us; the launch traced here: 131 us
  Pallas kernels  129 us (98%)
  local copies, waits for them, and re-layouts  2.06 us (2%)
    pallas_call x1, Pallas kernels, shards(): pl.pallas_call(kernel, out_shape=jax.ShapeDtypeStruct((ROWS, SLICE), BF),...  129 us

profile of v4, /device:TPU:1, one launch (start us, length us, event | category | flops | bytes accessed | tf_op | source)
XLA Modules:
  0.0 131.0 jit_solution(7894923264331905150)
XLA Ops:
  0.0 129.0 %joint_attention.1 = bf16[512,768]{1,0:T(8,128)(2,1)} custom-call(bf16[512,768]{1,0:T(8,128)(2,1)} %img_h.1, f32[3,3072]{1,0:T(4,128)} %mod.1, bf16[3072,384]{1,0:T(8,128)(2,1)} %wq_h.1, bf16[3072,384]{1,0:T(8,128)(2,1)} %wk_h.1, bf16[3072,384]{1,0:T(8,128)(2,1)} %wv_h.1, bf16[384,3072]{1,0:T(8,128)(2,1)} %wo_h.1, f32[1,128]{1,0:T(1,128)} %bitcast.2, ...), custom_call_target="tpu_custom_call" | custom-call | flops 12000000000 | bytes 20000000 | tf_op jit(solution)/shard_map/joint_attention/pallas_call | solution.py:674
  129.0 2.1 %copy.14 = bf16[512,768]{1,0:T(8,128)(2,1)} copy(bf16[512,768]{1,0:T(8,128)(2,1)} %joint_attention.1) | data formatting | bytes 1572864

commit v5 on v4

--- a/solution.py
+++ b/solution.py
@@ -311,6 +311,7 @@
             got(w_end.at[j, w_rows], W_A, j)
             for d in (1, 2, 3):
                 w_b(j, d).start()
+        start_near()
 
     for m in (1, 2):
         @pl.when(t != m)
@@ -437,9 +438,6 @@
             wait_w_b(j)
             for s in (0, 1):
                 w_c(j, s).start()
-        start_near()
-        for d in (1, 2, 3):
-            o_b(d).start()
         w_forward(0)
         w_forward(1)
         far_z(0, 0)
@@ -451,11 +449,10 @@
         w_share(1)
         far_z(1, 1)
         w_share(2)
-        wait_o_b()
-        for d in (1, 2, 3):
-            o_c(d).start()
         far_on(0)
         near_last()
+        for d in (1, 2, 3):
+            o_b(d).start()
         image_chunk(0)
         project(0, w_own, put_own)
 
@@ -559,6 +556,9 @@
         @pl.when((c == 1) & is_mid)
         def _():
             far_on(1)
+            wait_o_b()
+            for d in (1, 2, 3):
+                o_c(d).start()
 
         @pl.when((c == 2) & is_mid)
         def _():
@@ -575,8 +575,6 @@
     @pl.when(is_mid)
     def _():
         middle_chunk(NCH - 1)
-        wait_o_c()
-        o_d().start()
         far_rest()
 
         @pl.loop(0, NCH - 1)
@@ -584,6 +582,9 @@
             distant(c)
             finish(c)
 
+        wait_o_c()
+        o_d().start()
+
     @pl.when(is_end)
     def _():
         distant(NCH - 2)
@@ -603,16 +604,19 @@
         def _():
             relay(b - 1)
 
-            @pl.when(b == 8192 // KB - 1)
+            @pl.when(b == 2)
             def _():
                 got(w_o.at[pl.ds(1, 3), pl.ds(pl.multiple_of((1 - cc) * 192, 192), 192)], O_D)
-                project_out(0)
+
+            @pl.when(b > 1)
+            def _():
+                project_out(b - 2)
 
     finish(NCH - 1)
 
     @pl.when(is_mid)
     def _():
-        @pl.loop(1, NCH)
+        @pl.loop(2, NCH)
         def _(c):
             @pl.when(c == 2)
             def _():

time: 132 us -> 132 us (level)
  no operation moved by 1% of the time
where the time goes in v5:
time: 132 us
  Pallas kernels  130 us (98%)
  local copies, waits for them, and re-layouts  2.06 us (2%)
    pallas_call x1, Pallas kernels, shards(): pl.pallas_call(kernel, out_shape=jax.ShapeDtypeStruct((ROWS, SLICE), BF),...  130 us

profile of v5, /device:TPU:1, one launch (start us, length us, event | category | flops | bytes accessed | tf_op | source)
XLA Modules:
  0.0 132.1 jit_solution(12717902380652507717)
XLA Ops:
  0.0 130.0 %joint_attention.1 = bf16[512,768]{1,0:T(8,128)(2,1)} custom-call(bf16[512,768]{1,0:T(8,128)(2,1)} %img_h.1, f32[3,3072]{1,0:T(4,128)} %mod.1, bf16[3072,384]{1,0:T(8,128)(2,1)} %wq_h.1, bf16[3072,384]{1,0:T(8,128)(2,1)} %wk_h.1, bf16[3072,384]{1,0:T(8,128)(2,1)} %wv_h.1, bf16[384,3072]{1,0:T(8,128)(2,1)} %wo_h.1, f32[1,128]{1,0:T(1,128)} %bitcast.2, ...), custom_call_target="tpu_custom_call" | custom-call | flops 12000000000 | bytes 20000000 | tf_op jit(solution)/shard_map/joint_attention/pallas_call | solution.py:678
  130.0 2.1 %copy.14 = bf16[512,768]{1,0:T(8,128)(2,1)} copy(bf16[512,768]{1,0:T(8,128)(2,1)} %joint_attention.1) | data formatting | bytes 1572864
